TPU v7x, 32 devices: a whole 2x2x4 slice. The times are simulated.
32 devices in a mesh: row: 4 (over y, core), col: 8 (over z, x).
Axes of the slice: x: 2, y: 2, z: 4, core: 2. Of those that a mesh axis runs over, the one named last changes fastest.
Arguments:
- left: bfloat16 [8, 16, 512, 256], P('row', 'col'), may hold values from -0.11767578 to 0.11767578
- right: bfloat16 [8, 16, 512, 256], P('row', 'col'), may hold values from -6 to 6
- lower_inverse: bfloat16 [2, 512, 512], P(None, 'row'), as said below
- upper_inverse: bfloat16 [2, 512, 512], P(None, None, 'col'), as said below
- ranks: int32 [8, 16], P('row', 'col'), may hold values from 16 to 256, as said below
Outputs:
- right_out: bfloat16 [8, 16, 512, 256], P('row', 'col')
Inputs may be any that keep to these rules, and one draw needn't show every extreme that they name: Tile ranks: every row of `ranks` contains at least one entry equal to 256; all entries lie in 4..256. Each lower_inverse[k] is lower triangular with a positive diagonal. Each upper_inverse[k] is upper triangular with a positive diagonal.
All inputs are finite; a program needn't handle non-finite values.
Results may differ from a plain program's by a relative error of at most 0.009.
Values may be sent and summed in bfloat16 or wider, within the bound.
A program may use at most 64 MiB of HBM per device.

v0:
```python
import jax
import jax.numpy as jnp
from jax import lax
from jax.sharding import PartitionSpec as P


def broadcast(value, axis, source):
    kept = jnp.where(lax.axis_index(axis) == source, value, 0).astype(value.dtype)
    return lax.psum(kept, axis)


def update_tiles(
    left, right, col_left, col_right, row_left, row_right, tile_rows, tile_cols, panel
):
    core = jnp.einsum("abr,cbs->acrs", col_right, row_left, preferred_element_type=jnp.float32)
    intersection = jnp.einsum("acbr,abs->acrs", left, col_left, preferred_element_type=jnp.float32)
    mixed = jnp.einsum(
        "acrs,acst->acrt", intersection, core, precision=lax.Precision.HIGHEST
    ).astype(jnp.bfloat16)
    change = jnp.einsum("cbt,acrt->acbr", row_right, mixed, preferred_element_type=jnp.float32)
    fresh = (right.astype(jnp.float32) - change).astype(jnp.bfloat16)
    below = (tile_rows > panel)[:, None, None, None]
    trail = below & (tile_cols > panel)[None, :, None, None]
    on_panel = below & (tile_cols == panel)[None, :, None, None]
    kept = jnp.where(on_panel, col_right[:, None], right)
    return jnp.where(trail, fresh, kept)


def body(left, right, lower_inverse, upper_inverse, ranks):
    slots = lax.broadcasted_iota(jnp.int32, ranks.shape + (left.shape[3],), 2)
    keep = (slots < ranks[:, :, None]).astype(jnp.bfloat16)
    left = left * keep[:, :, None, :]
    right = right * keep[:, :, None, :]
    row_count = lax.axis_size("row")
    col_count = lax.axis_size("col")
    row_index = lax.axis_index("row")
    col_index = lax.axis_index("col")
    tile_rows = jnp.arange(left.shape[0], dtype=jnp.int32) * row_count + row_index
    tile_cols = jnp.arange(left.shape[1], dtype=jnp.int32) * col_count + col_index
    full_lower = lax.all_gather(lower_inverse, "row", axis=1, tiled=True)
    full_upper = lax.all_gather(upper_inverse, "col", axis=2, tiled=True)
    for panel in range(lower_inverse.shape[0]):

        def solve_column(factor):
            return jnp.einsum(
                "bc,abr->acr", full_upper[panel], factor, preferred_element_type=jnp.float32
            ).astype(jnp.bfloat16)

        def solve_row(factor):
            return jnp.einsum(
                "cb,jbr->jcr", full_lower[panel], factor, preferred_element_type=jnp.float32
            ).astype(jnp.bfloat16)

        solved_col = lax.cond(col_index == panel, solve_column, lambda factor: factor, right[:, 0])
        col_left, col_right = (
            broadcast(left[:, 0], "col", panel),
            broadcast(solved_col, "col", panel),
        )
        solved_row = lax.cond(row_index == panel, solve_row, lambda factor: factor, left[0])
        row_left, row_right = (
            broadcast(solved_row, "row", panel),
            broadcast(right[0], "row", panel),
        )
        right = update_tiles(
            left, right, col_left, col_right, row_left, row_right, tile_rows, tile_cols, panel
        )
    return right


def solution(mesh):
    placed = (
        P("row", "col", None, None),
        P("row", "col", None, None),
        P(None, "row", None),
        P(None, None, "col"),
        P("row", "col"),
    )
    return jax.shard_map(
        body, mesh=mesh, in_specs=placed, out_specs=P("row", "col", None, None), check_vma=False
    )
```

profile of v0, /device:TPU:0, one launch (start us, length us, event | category | flops | bytes accessed | tf_op | source)
XLA Modules:
  0.0 327.3 jit_solution(1950935950600516134)
XLA Ops:
  6.5 1.7 copy.21
  9.8 1.7 broadcast_multiply_fusion
  11.5 1.2 select_bitcast_fusion
  12.7 39.6 %all-gather.5.cloned.1.call-done = bf16[2,512,512]{1,0,2:T(2,128)(2,1)} async-done(((bf16[2,512,64]{1,0,2:T(2,128)(2,1)}), bf16[2,512,512]{1,0,2:T(2,128)(2,1)}) %all-gather.5.cloned.1.call-update) | async-done | bytes 1048592 | tf_op jit(solution)/shard_map/all_gather | solution.py:41
  52.4 5.2 %conditional.5 = (bf16[2,512,256]{1,2,0:T(8,128)(2,1)S(1)}) conditional(s32[]{:T(128)} %convert_element_type.73, (bf16[2,512,256]{2,1,0:T(8,128)(2,1)S(1)}) %tuple.40, (bf16[2,512,512]{1,0,2:T(2,128)(2,1)}, bf16[2,512,256]{2,1,0:T(8,128)(2,1)S(1)}) %tuple.30), branch_computations={%region_4.5_spmd, %region_5.6_spmd} | conditional | flops 268697600 | bytes 3670024 | solution.py:54
  52.4 3.7 %copy.23 = bf16[2,512,512]{2,1,0:T(8,128)(2,1)} copy(bf16[2,512,512]{1,0,2:T(2,128)(2,1)} %get-tuple-element.55) | data formatting | bytes 2097152 | tf_op jit(solution)/shard_map
  56.0 1.5 fusion.3
  57.5 0.9 broadcast_select_fusion.2
  58.8 0.9 fusion.17
  59.6 9.8 %all-gather.3.cloned.1.call-done = bf16[2,512,512]{2,1,0:T(8,128)(2,1)} async-done(((bf16[2,128,512]{2,1,0:T(8,128)(2,1)}), bf16[2,512,512]{2,1,0:T(8,128)(2,1)}) %all-gather.3.cloned.1.call-update) | async-done | bytes 1048592 | tf_op jit(solution)/shard_map/all_gather | solution.py:40
  69.4 1.5 conditional.4
  69.4 1.5 fusion
  71.0 0.8 broadcast_select_fusion.3
  72.0 79.4 %all-reduce.11.cloned.1.call-done = (bf16[2,512,256]{1,2,0:T(8,128)(2,1)}, bf16[2,512,256]{2,1,0:T(8,128)(2,1)}) async-done(((bf16[2,512,256]{1,2,0:T(8,128)(2,1)}, bf16[2,512,256]{2,1,0:T(8,128)(2,1)}), (bf16[2,512,256]{1,2,0:T(8,128)(2,1)}, bf16[2,512,256]{2,1,0:T(8,128)(2,1)})) %all-reduce.11.cloned.1.call-update) | async-done | bytes 1048592 | tf_op jit(solution)/shard_map/psum | solution.py:9
  151.4 2.1 copy.26
  153.5 1.6 fusion.24
  155.1 34.3 %all-reduce.15.cloned.1.call-done = (bf16[2,512,256]{2,1,0:T(8,128)(2,1)}, bf16[2,512,256]{1,2,0:T(8,128)(2,1)}) async-done(((bf16[2,512,256]{2,1,0:T(8,128)(2,1)}, bf16[2,512,256]{1,2,0:T(8,128)(2,1)}), (bf16[2,512,256]{2,1,0:T(8,128)(2,1)}, bf16[2,512,256]{1,2,0:T(8,128)(2,1)})) %all-reduce.15.cloned.1.call-update) | async-done | bytes 1048592 | tf_op jit(solution)/shard_map/psum | solution.py:9
  189.4 1.7 fusion.22
  191.9 1.2 convolution_convert_fusion.5
  194.0 0.8 slice_bitcast_fusion.4
  194.9 0.9 copy-done
  195.8 1.3 conditional.7
  195.8 1.3 copy.53
  197.1 0.8 broadcast_select_fusion
  198.1 0.8 broadcast_select_fusion.1
  199.4 0.9 fusion.16
  200.4 76.7 %all-reduce.9.cloned.1.call-done = (bf16[2,512,256]{1,2,0:T(8,128)(2,1)}, bf16[2,512,256]{2,1,0:T(8,128)(2,1)}) async-done(((bf16[2,512,256]{1,2,0:T(8,128)(2,1)}, bf16[2,512,256]{2,1,0:T(8,128)(2,1)}), (bf16[2,512,256]{1,2,0:T(8,128)(2,1)}, bf16[2,512,256]{2,1,0:T(8,128)(2,1)})) %all-reduce.9.cloned.1.call-update) | async-done | bytes 1048592 | tf_op jit(solution)/shard_map/psum | solution.py:9
  277.1 2.1 copy.33
  279.7 35.3 %all-reduce.13.cloned.1.call-done = (bf16[2,512,256]{2,1,0:T(8,128)(2,1)}, bf16[2,512,256]{1,2,0:T(8,128)(2,1)}) async-done(((bf16[2,512,256]{2,1,0:T(8,128)(2,1)}, bf16[2,512,256]{1,2,0:T(8,128)(2,1)}), (bf16[2,512,256]{2,1,0:T(8,128)(2,1)}, bf16[2,512,256]{1,2,0:T(8,128)(2,1)})) %all-reduce.13.cloned.1.call-update) | async-done | bytes 1048592 | tf_op jit(solution)/shard_map/psum | solution.py:9
  315.1 1.5 fusion.18
  317.4 1.2 convolution_convert_fusion.4
  318.9 1.6 fusion.11
  (49 shorter events, 6.2 us)
Async XLA Ops:
  6.5 45.8 %all-gather.5.cloned.1.call-start = ((), (), s32[]{:S(2)}) async-start(), calls=%async_computation.1 | async-start | bytes 1179648 | tf_op jit(solution)/shard_map/all_gather | solution.py:41
  8.3 61.2 %all-gather.3.cloned.1.call-start = ((), (), s32[]{:S(2)}) async-start(), calls=%async_computation | async-start | bytes 1310720 | tf_op jit(solution)/shard_map/all_gather | solution.py:40
  9.0 142.4 %all-reduce.11.cloned.1.call-start = ((), (), s32[]{:S(2)}) async-start(), calls=%async_computation.3 | async-start | bytes 2097152 | tf_op jit(solution)/shard_map/psum | solution.py:9
  11.5 47.2 %copy-start.1 = (bf16[2,2,512,256]{3,2,1,0:T(8,128)(2,1)}, bf16[2,2,512,256]{3,2,1,0:T(8,128)(2,1)S(1)}, u32[]{:S(2)}) copy-start(bf16[2,2,512,256]{3,2,1,0:T(8,128)(2,1)S(1)} %get-tuple-element.76) | copy-start | bytes 3145732
  58.4 131.0 %all-reduce.15.cloned.1.call-start = ((), (), s32[]{:S(2)}) async-start(), calls=%async_computation.5 | async-start | bytes 2097152 | tf_op jit(solution)/shard_map/psum | solution.py:9
  71.8 205.2 %all-reduce.9.cloned.1.call-start = ((), (), s32[]{:S(2)}) async-start(), calls=%async_computation.2 | async-start | bytes 2097152 | tf_op jit(solution)/shard_map/psum | solution.py:9
  191.9 1.2 copy-start.2
  191.9 1.3 copy-start.9
  191.9 1.5 copy-start.10
  194.0 1.8 copy-start.4
  194.0 1.8 copy-start
  198.0 117.1 %all-reduce.13.cloned.1.call-start = ((), (), s32[]{:S(2)}) async-start(), calls=%async_computation.4 | async-start | bytes 2097152 | tf_op jit(solution)/shard_map/psum | solution.py:9
  198.0 1.4 copy-start.5
  277.1 2.1 copy-start.7
  279.2 35.9 %copy-start.3 = (bf16[2,512,256]{1,2,0:T(8,128)(2,1)S(1)}, bf16[2,512,256]{1,2,0:T(8,128)(2,1)}, u32[]{:S(2)}) copy-start(bf16[2,512,256]{1,2,0:T(8,128)(2,1)} %get-tuple-element.65) | copy-start | bytes 1572868
  317.4 1.2 copy-start.6
  317.4 1.3 copy-start.8
  317.4 1.5 copy-start.11
Sparse Core Ops, SparseCore 0:
  9.5 42.8 all-gather.4
  53.9 15.4 all-gather.2
  73.0 78.3 all-reduce.10
  153.9 35.4 all-reduce.14
  198.1 78.9 all-reduce.8
  279.5 35.4 all-reduce.12
where the time goes:
time: 328 us; the launch traced here: 327 us
  waiting for transfers between devices  276 us (84%)
  local copies, waits for them, and re-layouts  15.6 us (5%)
  between operations  13.7 us (4%)
  matrix products  12.8 us (4%)
  other arithmetic  8.93 us (3%)
    psum x4, waiting for transfers between devices, broadcast(): return lax.psum(kept, axis)  226 us
    all_gather x1, waiting for transfers between devices, body(): full_upper = lax.all_gather(upper_inverse, 'col', axis=2, tiled=True)  39.6 us
    all_gather x1, waiting for transfers between devices, body(): full_lower = lax.all_gather(lower_inverse, 'row', axis=1, tiled=True)  9.83 us
  transfers between devices with their start and end apart: 6, of which 6 were waited for; matrix products, arithmetic and copies ran while one was open for 6% of the time, Pallas kernels for 0%

commit v1 on v0

--- a/solution.py
+++ b/solution.py
@@ -37,7 +37,18 @@
     col_index = lax.axis_index("col")
     tile_rows = jnp.arange(left.shape[0], dtype=jnp.int32) * row_count + row_index
     tile_cols = jnp.arange(left.shape[1], dtype=jnp.int32) * col_count + col_index
-    full_lower = lax.all_gather(lower_inverse, "row", axis=1, tiled=True)
+    ways = lax.axis_size("row")
+    up = [(d, (d + 1) % ways) for d in range(ways)]
+    down = [(d, (d - 1) % ways) for d in range(ways)]
+    earlier, later = ([lower_inverse], [lower_inverse])
+    for _ in range(ways // 2):
+        earlier.append(lax.ppermute(earlier[-1], "row", up))
+    for _ in range((ways - 1) // 2):
+        later.append(lax.ppermute(later[-1], "row", down))
+    line = jnp.concatenate([*earlier[::-1], *later[1:]], axis=1)
+    full_lower = jnp.roll(
+        line, (lax.axis_index("row") - ways // 2) * lower_inverse.shape[1], axis=1
+    )
     full_upper = lax.all_gather(upper_inverse, "col", axis=2, tiled=True)
     for panel in range(lower_inverse.shape[0]):
 

time: 328 us -> 310 us (0.945)
  waiting for transfers between devices: 276 us -> 242 us
  local copies, waits for them, and re-layouts: 15.6 us -> 27 us
  starting transfers between devices: 0.21 us -> 5.2 us
    psum x4, waiting for transfers between devices: 226 us -> 213 us  [broadcast(): return lax.psum(kept, axis)]
    all_gather x1, waiting for transfers between devices: 39.6 us -> 27.7 us  [body(): full_upper = lax.all_gather(upper_inverse, 'col', axis=2, tiled=True)]
    all_gather x1 -> x0, waiting for transfers between devices: 9.83 us -> none  [body(): full_lower = lax.all_gather(lower_inverse, 'row', axis=1, tiled=True)]
    unnamed x25 -> x34, local copies, waits for them, and re-layouts: 3.88 us -> 11.1 us
    ppermute x0 -> x3, starting transfers between devices: none -> 5.03 us  [the longest x2 3.01 us: body(): earlier.append(lax.ppermute(earlier[-1], 'row', up))]
  transfers between devices with their start and end apart: 6 -> 8, of which waited for: 6 -> 7; matrix products, arithmetic and copies ran while one was open for 6% -> 11% of each run, Pallas kernels for 0% -> 0%
where the time goes in v1:
time: 310 us; the launch traced here: 309 us
  waiting for transfers between devices  242 us (78%)
  local copies, waits for them, and re-layouts  27 us (9%)
  between operations  13.4 us (4%)
  matrix products  12.9 us (4%)
  other arithmetic  8.86 us (3%)
  starting transfers between devices  5.2 us (2%)
    psum x4, waiting for transfers between devices, broadcast(): return lax.psum(kept, axis)  213 us
    all_gather x1, waiting for transfers between devices, body(): full_upper = lax.all_gather(upper_inverse, 'col', axis=2, tiled=True)  27.7 us
    unnamed x34, local copies, waits for them, and re-layouts  11.1 us
    select_n x7, other arithmetic, broadcast(): jnp.where(lax.axis_index(axis) == source, value, 0).astype(value.dtype)  6.25 us
  transfers between devices with their start and end apart: 8, of which 7 were waited for; matrix products, arithmetic and copies ran while one was open for 11% of the time, Pallas kernels for 0%

profile of v1, /device:TPU:0, one launch (start us, length us, event | category | flops | bytes accessed | tf_op | source)
XLA Modules:
  0.0 309.3 jit_solution(7584305501647721036)
XLA Ops:
  6.5 1.7 copy.21
  8.8 2.0 collective-permute-start.2
  11.6 1.7 broadcast_multiply_fusion
  13.3 1.2 select_bitcast_fusion
  15.3 2.5 collective-permute-start.1
  18.6 1.3 copy.19
  21.4 1.7 constant_dynamic-update-slice_fusion.7
  23.1 1.7 constant_dynamic-update-slice_fusion.6
  24.7 27.7 %all-gather.2.cloned.1.call-done = bf16[2,512,512]{1,0,2:T(2,128)(2,1)} async-done(((bf16[2,512,64]{1,0,2:T(2,128)(2,1)}), bf16[2,512,512]{1,0,2:T(2,128)(2,1)}) %all-gather.2.cloned.1.call-update) | async-done | bytes 1048592 | tf_op jit(solution)/shard_map/all_gather | solution.py:52
  52.4 5.2 %conditional.5 = (bf16[2,512,256]{1,2,0:T(8,128)(2,1)S(1)}) conditional(s32[]{:T(128)} %convert_element_type.73, (bf16[2,512,256]{2,1,0:T(8,128)(2,1)S(1)}) %tuple.40, (bf16[2,512,512]{1,0,2:T(2,128)(2,1)}, bf16[2,512,256]{2,1,0:T(8,128)(2,1)S(1)}) %tuple.30), branch_computations={%region_4.5_spmd, %region_5.6_spmd} | conditional | flops 268697600 | bytes 3670024 | solution.py:65
  52.4 3.7 %copy.23 = bf16[2,512,512]{2,1,0:T(8,128)(2,1)} copy(bf16[2,512,512]{1,0,2:T(2,128)(2,1)} %get-tuple-element.55) | data formatting | bytes 2097152 | tf_op jit(solution)/shard_map
  56.1 1.5 fusion.3
  60.0 1.7 constant_dynamic-update-slice_fusion.3
  61.8 1.7 constant_dynamic-update-slice_fusion.2
  65.0 2.3 constant_dynamic-slice_fusion
  67.3 1.5 conditional.4
  67.3 1.5 fusion
  69.8 64.5 %all-reduce.11.cloned.1.call-done = (bf16[2,512,256]{1,2,0:T(8,128)(2,1)}, bf16[2,512,256]{2,1,0:T(8,128)(2,1)}) async-done(((bf16[2,512,256]{1,2,0:T(8,128)(2,1)}, bf16[2,512,256]{2,1,0:T(8,128)(2,1)}), (bf16[2,512,256]{1,2,0:T(8,128)(2,1)}, bf16[2,512,256]{2,1,0:T(8,128)(2,1)})) %all-reduce.11.cloned.1.call-update) | async-done | bytes 1048592 | tf_op jit(solution)/shard_map/psum | solution.py:9
  134.2 2.0 copy.26
  136.3 36.1 %all-reduce.15.cloned.1.call-done = (bf16[2,512,256]{2,1,0:T(8,128)(2,1)}, bf16[2,512,256]{1,2,0:T(8,128)(2,1)}) async-done(((bf16[2,512,256]{2,1,0:T(8,128)(2,1)}, bf16[2,512,256]{1,2,0:T(8,128)(2,1)}), (bf16[2,512,256]{2,1,0:T(8,128)(2,1)}, bf16[2,512,256]{1,2,0:T(8,128)(2,1)})) %all-reduce.15.cloned.1.call-update) | async-done | bytes 1048592 | tf_op jit(solution)/shard_map/psum | solution.py:9
  172.4 1.7 fusion.22
  175.5 1.2 convolution_convert_fusion.5
  177.3 0.9 slice_bitcast_fusion.4
  178.5 1.3 conditional.7
  178.5 1.3 copy.53
  182.7 76.9 %all-reduce.9.cloned.1.call-done = (bf16[2,512,256]{1,2,0:T(8,128)(2,1)}, bf16[2,512,256]{2,1,0:T(8,128)(2,1)}) async-done(((bf16[2,512,256]{1,2,0:T(8,128)(2,1)}, bf16[2,512,256]{2,1,0:T(8,128)(2,1)}), (bf16[2,512,256]{1,2,0:T(8,128)(2,1)}, bf16[2,512,256]{2,1,0:T(8,128)(2,1)})) %all-reduce.9.cloned.1.call-update) | async-done | bytes 1048592 | tf_op jit(solution)/shard_map/psum | solution.py:9
  259.6 1.3 copy.33
  261.0 1.6 fusion.20
  262.5 35.1 %all-reduce.13.cloned.1.call-done = (bf16[2,512,256]{2,1,0:T(8,128)(2,1)}, bf16[2,512,256]{1,2,0:T(8,128)(2,1)}) async-done(((bf16[2,512,256]{2,1,0:T(8,128)(2,1)}, bf16[2,512,256]{1,2,0:T(8,128)(2,1)}), (bf16[2,512,256]{2,1,0:T(8,128)(2,1)}, bf16[2,512,256]{1,2,0:T(8,128)(2,1)})) %all-reduce.13.cloned.1.call-update) | async-done | bytes 1048592 | tf_op jit(solution)/shard_map/psum | solution.py:9
  297.6 1.5 fusion.18
  300.0 1.2 convolution_convert_fusion.4
  301.1 1.6 fusion.11
  (63 shorter events, 15.3 us)
Async XLA Ops:
  6.5 45.9 %all-gather.2.cloned.1.call-start = ((), (), s32[]{:S(2)}) async-start(), calls=%async_computation | async-start | bytes 1179648 | tf_op jit(solution)/shard_map/all_gather | solution.py:52
  8.2 126.0 %all-reduce.11.cloned.1.call-start = ((), (), s32[]{:S(2)}) async-start(), calls=%async_computation.2 | async-start | bytes 2097152 | tf_op jit(solution)/shard_map/psum | solution.py:9
  8.3 7.0 %collective-permute-start = (bf16[2,128,512]{2,1,0:T(8,128)(2,1)}, bf16[2,128,512]{2,1,0:T(8,128)(2,1)}, u32[]{:S(2)}, u32[]{:S(2)}) collective-permute-start(bf16[2,128,512]{2,1,0:T(8,128)(2,1)} %param.15), channel_id=1, source_target_pairs={{0,8},{8,16},{16,24},{24,0},{1,9},{9,17},{17,25},{25,1},{2,10},{10... | collective-permute-start | bytes 786440 | tf_op jit(solution)/shard_map/ppermute | solution.py:45
  8.8 50.5 %collective-permute-start.2 = (bf16[2,128,512]{2,1,0:T(8,128)(2,1)}, bf16[2,128,512]{2,1,0:T(8,128)(2,1)S(1)}, u32[]{:S(2)}, u32[]{:S(2)}) collective-permute-start(bf16[2,128,512]{2,1,0:T(8,128)(2,1)} %param.15), channel_id=1, source_target_pairs={{0,24},{8,0},{16,8},{24,16},{1,25},{9,1},{17,9},{25,17},{2,26},{10... | collective-permute-start | bytes 786440 | tf_op jit(solution)/shard_map/ppermute | solution.py:47
  13.2 6.6 %copy-start.1 = (bf16[2,2,512,256]{3,2,1,0:T(8,128)(2,1)}, bf16[2,2,512,256]{3,2,1,0:T(8,128)(2,1)S(1)}, u32[]{:S(2)}) copy-start(bf16[2,2,512,256]{3,2,1,0:T(8,128)(2,1)S(1)} %get-tuple-element.76) | copy-start | bytes 3145732
  15.3 6.1 %collective-permute-start.1 = (bf16[2,128,512]{2,1,0:T(8,128)(2,1)}, bf16[2,128,512]{2,1,0:T(8,128)(2,1)}, u32[]{:S(2)}, u32[]{:S(2)}) collective-permute-start(bf16[2,128,512]{2,1,0:T(8,128)(2,1)} %collective-permute-done), channel_id=1, source_target_pairs={{0,8},{8,16},{16,24},{24,0},{1,9},{9,17},{17,25},{25,1},{2,10},{10... | collective-permute-start | bytes 786440 | tf_op jit(solution)/shard_map/ppermute | solution.py:45
  57.6 1.0 copy-start.5
  58.5 113.9 %all-reduce.15.cloned.1.call-start = ((), (), s32[]{:S(2)}) async-start(), calls=%async_computation.4 | async-start | bytes 2097152 | tf_op jit(solution)/shard_map/psum | solution.py:9
  60.0 7.2 %copy-start.3 = (bf16[2,512,256]{2,1,0:T(8,128)(2,1)S(1)}, bf16[2,512,256]{2,1,0:T(8,128)(2,1)}, u32[]{:S(2)}) copy-start(bf16[2,512,256]{2,1,0:T(8,128)(2,1)} %slice_bitcast_fusion.6) | copy-start | bytes 1572868
  69.6 190.0 %all-reduce.9.cloned.1.call-start = ((), (), s32[]{:S(2)}) async-start(), calls=%async_computation.1 | async-start | bytes 2097152 | tf_op jit(solution)/shard_map/psum | solution.py:9
  172.4 2.6 copy-start.9
  174.9 1.7 copy-start.2
  174.9 1.7 copy-start.10
  175.0 1.7 copy-start.11
  176.7 1.6 copy-start
  177.3 1.1 copy-start.6
  180.6 1.2 copy-start.7
  180.6 117.0 %all-reduce.13.cloned.1.call-start = ((), (), s32[]{:S(2)}) async-start(), calls=%async_computation.3 | async-start | bytes 2097152 | tf_op jit(solution)/shard_map/psum | solution.py:9
  259.6 38.0 %copy-start.4 = (bf16[2,512,256]{1,2,0:T(8,128)(2,1)S(1)}, bf16[2,512,256]{1,2,0:T(8,128)(2,1)}, u32[]{:S(2)}) copy-start(bf16[2,512,256]{1,2,0:T(8,128)(2,1)} %get-tuple-element.65) | copy-start | bytes 1572868
  299.1 2.0 copy-start.8
  299.1 2.0 copy-start.12
Sparse Core Ops, SparseCore 0:
  9.5 42.8 all-gather.1
  58.6 75.6 all-reduce.10
  136.8 35.4 all-reduce.14
  180.7 78.8 all-reduce.8
  262.1 35.4 all-reduce.12
